TPU v7x, 1024 devices: a whole 4x8x16 slice. The times are simulated.
1024 devices in a mesh: group: 32 (over y, x_lo, core), table: 16 (over z), batch: 2 (over x_hi).
Axes of the slice: x: 4 (x_hi: 2, x_lo: 2; x = x_hi * 2 + x_lo), y: 8, z: 16, core: 2. Of those that a mesh axis runs over, the one named last changes fastest.
Arguments:
- features_in: bfloat16 [64, 2048, 3456], P(('group', 'batch'), 'table'), may hold values from -6 to 6
- cross_cot: bfloat16 [64, 2048, 3456], P(('group', 'batch'), 'table'), may hold values from -6 to 6
- cross_down: bfloat16 [3456, 512], replicated, may hold values from -0.109375 to 0.109375
- cross_up: bfloat16 [512, 3456], replicated, may hold values from -0.25 to 0.25
- cross_bias: float32 [3456], replicated, may hold values from -3 to 3
- lookups: int32 [16, 64, 2048, 2], P('table', ('group', 'batch')), may hold values from 0 to 8191, as said below
Outputs:
- bottom_grad: bfloat16 [64, 2048, 128], P(('group', 'batch'), 'table')
- bias_grad: float32 [3456], replicated
- row_grad: float32 [16, 8192, 128], P('table', ('group', 'batch'))
Inputs may be any that keep to these rules, and one draw needn't show every extreme that they name: Block b owns rows b * 128 to (b + 1) * 128 - 1 of each table. In each feature, the 4096 lookups of one block fall on the rows of any one block at most 96 times, and in each feature one block's rows receive exactly 96 lookups from every block.
All inputs are finite; a program needn't handle non-finite values.
Results may differ from a plain program's by a relative error of at most 0.012.
Values may be sent and summed in bfloat16 or wider, within the bound.
A program may use at most 64 MiB of HBM per device.

v0:
```python
import jax
import jax.numpy as jnp
from jax import lax
from jax.sharding import PartitionSpec as P

EMB = 128
BOTTOM = 128
ROWS_DEV = 128
POOL = 2


def rows_of(values, row_ids, count):
    local = row_ids
    inside = (local >= 0) & (local < count)
    local = jnp.where(inside, local, count).reshape(-1)
    spread = jnp.broadcast_to(
        values.astype(jnp.float32)[:, None, :], (values.shape[0], POOL, EMB)
    ).reshape(-1, EMB)
    return jax.ops.segment_sum(spread, local, num_segments=count + 1)[:count]


def body(features_in, cross_cot, cross_down, cross_up, cross_bias, lookups):
    inputs = features_in[0]
    cotan = cross_cot[0]
    low = jnp.dot(inputs, cross_down, preferred_element_type=jnp.float32).astype(jnp.bfloat16)
    gate = jnp.dot(low, cross_up, preferred_element_type=jnp.float32) + cross_bias
    cot_wide = cotan.astype(jnp.float32)
    gate_grad = cot_wide * inputs.astype(jnp.float32)
    bias_grad = lax.psum(jnp.sum(gate_grad, 0), ("group", "table", "batch"))
    low_grad = jnp.dot(
        gate_grad.astype(jnp.bfloat16), cross_up.T, preferred_element_type=jnp.float32
    ).astype(jnp.bfloat16)
    input_grad = (
        cot_wide * (gate + 1.0)
        + jnp.dot(low_grad, cross_down.T, preferred_element_type=jnp.float32)
    ).astype(jnp.bfloat16)
    nfeat = lax.axis_size("table")
    samples = inputs.shape[0]
    pooled = input_grad[:, BOTTOM : BOTTOM + nfeat * EMB].reshape(samples, nfeat, EMB)
    arrived = lax.all_to_all(pooled, "table", split_axis=1, concat_axis=0, tiled=True)
    values = arrived[:, 0, :]
    own_ids = lookups[0, 0]
    row_grad = lax.psum_scatter(
        rows_of(values, own_ids, ROWS_DEV * lax.axis_size(("group", "batch"))),
        ("group", "batch"),
        scatter_dimension=0,
        tiled=True,
    )
    return (input_grad[None, :, :BOTTOM], bias_grad, row_grad[None])


def solution(mesh):
    placed = (
        P(("group", "batch"), "table", None),
        P(("group", "batch"), "table", None),
        P(),
        P(),
        P(),
        P("table", ("group", "batch"), None, None),
    )
    return jax.shard_map(
        body,
        mesh=mesh,
        in_specs=placed,
        out_specs=(P(("group", "batch"), "table", None), P(), P("table", ("group", "batch"), None)),
        check_vma=False,
    )
```

profile of v0, /device:TPU:1, one launch (start us, length us, event | category | flops | bytes accessed | tf_op | source)
XLA Modules:
  0.0 378.4 jit_solution(5692267525103518761)
XLA Ops:
  7.2 0.0 copy-start
  7.2 2.0 copy-done
  9.2 5.0 %fusion.1 = f32[128,3456]{1,0:T(8,128)} fusion(bf16[512,3456]{1,0:T(8,128)(2,1)S(1)} %copy-done, bf16[3456,512]{1,0:T(8,128)(2,1)} %param.8, bf16[1,128,3456]{2,1,0:T(8,128)(2,1)} %param.7, bf16[1,128,3456]{2,1,0:T(8,128)(2,1)} %param.6, f32[3456]{0:T(1024)} %param.10), kind=kOutput, calls=%fused_computation.4 | convolution fusion | flops 907804672 | bytes 10630656 | tf_op jit(solution)/shard_map/dot_general | solution.py:26
  14.1 0.0 copy-start.1
  14.1 6.1 %fusion.2 = bf16[128,3456]{1,0:T(8,128)(2,1)} fusion(f32[128,3456]{1,0:T(8,128)} %fusion.1, bf16[3456,512]{1,0:T(8,128)(2,1)} %param.8, bf16[512,3456]{1,0:T(8,128)(2,1)S(1)} %copy-done, bf16[1,128,3456]{2,1,0:T(8,128)(2,1)} %param.7, bf16[1,128,3456]{2,1,0:T(8,128)(2,1)} %param.6), kind=kOutput, calls=%fused_computation.5 | convolution fusion | flops 908689408 | bytes 11501568 | tf_op jit(solution)/shard_map/dot_general | solution.py:35
  20.3 2.0 copy_bitcast_fusion
  22.3 19.5 %all-to-all-start = ((bf16[128,16,128]{2,0,1:T(8,128)(2,1)}), bf16[128,16,128]{2,0,1:T(8,128)(2,1)}, u32[]{:S(2)}, u32[]{:S(2)}) async-start(bf16[128,16,128]{2,0,1:T(8,128)(2,1)} %copy_bitcast_fusion), calls=%async_computation | async-start | bytes 1048576 | tf_op jit(solution)/shard_map/all_to_all | solution.py:40
  41.7 0.0 reduce-scatter.2.cloned.1.call-start
  41.8 0.0 copy-done.1
  41.8 1.4 copy.9
  43.2 1.8 squeeze.9
  45.0 0.6 and_select_fusion
  45.6 19.0 %all-to-all-done = bf16[128,16,128]{2,0,1:T(8,128)(2,1)} async-done(((bf16[128,16,128]{2,0,1:T(8,128)(2,1)}), bf16[128,16,128]{2,0,1:T(8,128)(2,1)}, u32[]{:S(2)}, u32[]{:S(2)}) %all-to-all-start) | async-done | bytes 524320 | tf_op jit(solution)/shard_map/all_to_all | solution.py:40
  64.6 1.1 bitcast_convert_fusion
  65.7 1.8 broadcast_in_dim.20
  67.5 24.8 %scatter_custom_fusion = f32[8193,128]{1,0:T(8,128)} fusion(s32[4096]{0:T(1024)} %bitcast.43, f32[4096,128]{1,0:T(8,128)} %bitcast.42, f32[]{:T(128)} %constant.5.clone.1), kind=kCustom, calls=%fused_computation.7 | custom fusion | flops 524288 | bytes 4195328 | tf_op jit(solution)/shard_map/scatter-add | solution.py:19
  92.3 4.4 %slice.14 = f32[8192,128]{1,0:T(8,128)} slice(f32[8193,128]{1,0:T(8,128)} %scatter_custom_fusion), slice={[0:8192], [0:128]} | slice | bytes 8388608 | tf_op jit(solution)/shard_map/slice | solution.py:19
  96.8 0.0 reduce-scatter.2.cloned.1.call-update
  96.8 1.7 fusion.5
  98.5 130.0 %psum.7 = f32[3456]{0:T(1024)} all-reduce(f32[3456]{0:T(1024)S(1)} %fusion.5), channel_id=1, replica_groups=mesh['group'=32,'table'=16,'batch'=2] {'group','table','batch'}, use_global_device_ids=true, to_apply=%region_1.0 | all-reduce | flops 3456 | bytes 27648 | tf_op jit(solution)/shard_map/psum | solution.py:29
  228.5 1.4 slice_bitcast_fusion.1
  229.8 141.7 %reduce-scatter.2.cloned.1.call-done = f32[128,128]{1,0:T(8,128)} async-done(((f32[8192,128]{1,0:T(8,128)}), f32[128,128]{1,0:T(8,128)}) %reduce-scatter.2.cloned.1.call-update) | async-done | bytes 65552 | tf_op jit(solution)/shard_map/reduce_scatter | solution.py:43
Async XLA Ops:
  7.2 2.0 copy-start
  14.1 27.6 %copy-start.1 = (s32[1,1,2048,2]{2,3,1,0:T(2,128)S(1)}, s32[1,1,2048,2]{2,3,1,0:T(2,128)}, u32[]{:S(2)}) copy-start(s32[1,1,2048,2]{2,3,1,0:T(2,128)} %param.11) | copy-start | bytes 49156
  22.3 42.4 %all-to-all-start = ((bf16[128,16,128]{2,0,1:T(8,128)(2,1)}), bf16[128,16,128]{2,0,1:T(8,128)(2,1)}, u32[]{:S(2)}, u32[]{:S(2)}) async-start(bf16[128,16,128]{2,0,1:T(8,128)(2,1)} %copy_bitcast_fusion), calls=%async_computation | async-start | bytes 1048576 | tf_op jit(solution)/shard_map/all_to_all | solution.py:40
  41.7 329.8 %reduce-scatter.2.cloned.1.call-start = ((), (), s32[]{:S(2)}) async-start(), calls=%async_computation.2 | async-start | bytes 4259840 | tf_op jit(solution)/shard_map/reduce_scatter | solution.py:43
Sparse Core Ops, SparseCore 0:
  96.9 274.6 reduce-scatter.1
where the time goes:
time: 380 us; the launch traced here: 378 us
  waiting for transfers between devices  161 us (42%)
  blocking collectives  130 us (34%)
  other arithmetic  28.3 us (7%)
  starting transfers between devices  19.5 us (5%)
  local copies, waits for them, and re-layouts  14.8 us (4%)
  between operations  14.1 us (4%)
  matrix products  11.1 us (3%)
    reduce_scatter x1, waiting for transfers between devices, body(): lax.psum_scatter(rows_of(values, own_ids, ROWS_DEV * lax.axis_size(('grou...  142 us
    psum x1, blocking collectives, body(): bias_grad = lax.psum(jnp.sum(gate_grad, 0), ('group', 'table', 'batch'))  130 us
    scatter-add x1, other arithmetic, rows_of(): return jax.ops.segment_sum(spread, local, num_segments=count + 1)[:count]  24.8 us
    all_to_all x1, starting transfers between devices, body(): lax.all_to_all(pooled, 'table', split_axis=1, concat_axis=0, tiled=True)  19.5 us
    all_to_all x1, waiting for transfers between devices, body(): lax.all_to_all(pooled, 'table', split_axis=1, concat_axis=0, tiled=True)  19 us
  transfers between devices with their start and end apart: 2, of which 2 were waited for; matrix products, arithmetic and copies ran while one was open for 2% of the time, Pallas kernels for 0%

commit v1 on v0

v1 whole, which is shorter than its diff:
```python
import functools

import jax
import jax.numpy as jnp
from jax import lax
from jax.experimental import pallas as pl
from jax.experimental.pallas import tpu as pltpu
from jax.sharding import PartitionSpec as P

MESH = pl.DeviceIdType.MESH
F32 = jnp.float32
BF16 = jnp.bfloat16
EMB = 128
ROWS_DEV = 128
XLO = 2
CORES = 2
KCHUNK = 384


def offset_of(step, size):
    half = (step + 1) // 2
    odd = step % 2
    return size // 2 + half * (1 - 2 * odd)


def kernel(
    sizes,
    feat_hbm, cot_hbm, down_hbm, up_hbm, bias_ref, ids_ref,
    bottom_ref, bias_out, row_out,
    feat, cot, down, up, low, low_grad, low_acc, grad_acc,
    pooled, vals, ids, hi, lo, acc,
    xs, xr, ys, yr,
    bias_part, bias_z, bias_c, bias_x, bias_y, bias_all,
    load_sem, ids_sem, zs_sem, zr_sem, fs_sem, fr_sem, xs_sem, xr_sem, ys_sem, yr_sem,
    bzs_sem, bzr_sem, bc_sem, bxs_sem, bxr_sem, bys_sem, byr_sem, bas_sem, bar_sem,
):
    ny, nx, nz = sizes
    width = feat.shape[1]
    chunks = width // KCHUNK
    group = lax.axis_index("group")
    x_hi = lax.axis_index("batch")
    z = lax.axis_index("table")
    y = group // (XLO * CORES)
    x_lo = (group // CORES) % XLO
    core = group % CORES
    x = x_hi * XLO + x_lo

    def device(xx, yy, zz, cc):
        return {"group": (yy * XLO + xx % XLO) * CORES + cc, "table": zz, "batch": xx // XLO}

    sibling = device(x, y, z, 1 - core)

    def x_peer(offset):
        return device((x + offset) % nx, y, z, core)

    def y_peer(offset):
        return device(x, (y + offset) % ny, z, core)

    def z_peer(offset):
        return device(x, y, (z + offset) % nz, core)

    def remote(src, dst, send, recv, target):
        return pltpu.make_async_remote_copy(
            src_ref=src, dst_ref=dst, send_sem=send, recv_sem=recv, device_id=target, device_id_type=MESH
        )

    barrier = pltpu.get_barrier_semaphore()

    def greet(target):
        pl.semaphore_signal(barrier, inc=1, device_id=target, device_id_type=MESH)

    greet(sibling)
    lax.fori_loop(1, nx, lambda i, c: (greet(x_peer(i)), c)[1], 0)
    lax.fori_loop(1, ny, lambda i, c: (greet(y_peer(i)), c)[1], 0)
    lax.fori_loop(1, nz, lambda i, c: (greet(z_peer(i)), c)[1], 0)

    def loads(k):
        cols = pl.ds(k * KCHUNK, KCHUNK)
        return (
            pltpu.make_async_copy(feat_hbm.at[:, cols], feat.at[:, cols], load_sem.at[0, k]),
            pltpu.make_async_copy(cot_hbm.at[:, cols], cot.at[:, cols], load_sem.at[1, k]),
            pltpu.make_async_copy(down_hbm.at[cols, :], down.at[cols, :], load_sem.at[2, k]),
            pltpu.make_async_copy(up_hbm.at[:, cols], up.at[:, cols], load_sem.at[3, k]),
        )

    for k in range(chunks):
        for copy in loads(k):
            copy.start()

    acc[...] = jnp.zeros_like(acc)
    bias_part[...] = jnp.zeros_like(bias_part)

    for k in range(chunks):
        for copy in loads(k):
            copy.wait()
        cols = slice(k * KCHUNK, (k + 1) * KCHUNK)
        part_in = feat[:, cols]
        gate_grad = cot[:, cols].astype(F32) * part_in.astype(F32)
        sums = jnp.sum(gate_grad, 0, keepdims=True)
        for j in range(KCHUNK // 128):
            g = k * (KCHUNK // 128) + j
            bias_part[g // 2, g % 2 : g % 2 + 1, :] = sums[:, j * 128 : (j + 1) * 128]
        first = jnp.dot(part_in, down[cols, :], preferred_element_type=F32)
        second = lax.dot_general(
            gate_grad.astype(BF16), up[:, cols], (((1,), (1,)), ((), ())), preferred_element_type=F32
        )
        if k == 0:
            low_acc[...] = first
            grad_acc[...] = second
        else:
            low_acc[...] += first
            grad_acc[...] += second
    low[...] = low_acc[...].astype(BF16)
    low_grad[...] = grad_acc[...].astype(BF16)

    pl.semaphore_wait(barrier, 1 + (nx - 1) + (ny - 1) + (nz - 1))

    ids_copy = remote(ids_ref, ids.at[core], ids_sem.at[0], ids_sem.at[1], sibling)
    ids_copy.start()
    ids[core] = ids_ref[...]

    def columns(start):
        cols = pl.ds(pl.multiple_of(start, 128), 128)
        gate = jnp.dot(low[...], up[:, cols], preferred_element_type=F32) + bias_ref[:, cols]
        back = lax.dot_general(
            low_grad[...], down[cols, :], (((1,), (1,)), ((), ())), preferred_element_type=F32
        )
        return (cot[:, cols].astype(F32) * (gate + 1.0) + back).astype(BF16)

    mine = pl.ds(pl.multiple_of(core * 128, 128), 128)

    def z_copy(step):
        offset = offset_of(step, nz)
        return remote(
            pooled.at[step], vals.at[z, mine], zs_sem.at[step], zr_sem.at[z], z_peer(offset)
        )

    def z_arrival(source):
        return remote(pooled.at[0], vals.at[source, mine], zs_sem.at[0], zr_sem.at[source], sibling)

    def bias_z_copy(step):
        offset = offset_of(step, nz)
        return remote(
            bias_part.at[(z + offset) % nz], bias_z.at[z], bzs_sem.at[step], bzr_sem.at[z], z_peer(offset)
        )

    def send_feature(step, carry):
        feature = (z + offset_of(step, nz)) % nz
        pooled[step] = columns(128 + feature * 128)
        z_copy(step).start()
        bias_z_copy(step).start()
        return carry

    send_feature(0, 0)

    def send_two(pair, carry):
        send_feature(2 * pair + 1, carry)
        send_feature(2 * pair + 2, carry)
        return carry

    lax.fori_loop(0, nz // 2 - 1, send_two, 0)
    vals[z, mine] = columns(128 + z * 128)

    def forward(source):
        place = vals.at[source, mine]
        return remote(place, place, fs_sem.at[source], fr_sem.at[source], sibling)

    def forwarded(source):
        place = vals.at[source, pl.ds(pl.multiple_of((1 - core) * 128, 128), 128)]
        return remote(place, place, fs_sem.at[source], fr_sem.at[source], sibling)

    forward(z).start()
    bottom_ref[...] = columns(0)

    remote(ids_ref, ids.at[1 - core], ids_sem.at[0], ids_sem.at[1], sibling).wait_recv()

    def split_ids(zz, carry):
        part = pl.ds(pl.multiple_of(zz * 128, 128), 128)
        for c in range(CORES):
            row = ids[c, :, part]
            block = row >> 7
            xx = (block & 1) * XLO + ((block >> 2) & 1)
            tile = xx * ny + (block >> 3)
            hi[zz, :, c * 128 : (c + 1) * 128] = jnp.where(((block >> 1) & 1) == core, tile, -1)
            lo[zz, :, c * 128 : (c + 1) * 128] = row & 127
        return carry

    lax.fori_loop(0, nz, split_ids, 0)

    def add_rows(source):
        value = vals[source]
        tile_of, inner = hi[source], lo[source]
        rows = lax.broadcasted_iota(jnp.int32, (ROWS_DEV, 256), 0).astype(F32).astype(BF16)
        one, zero = jnp.ones((), BF16), jnp.zeros((), BF16)
        for t in range(nx * ny):
            hit = jnp.where(tile_of == t, inner, -1).astype(F32).astype(BF16)
            onehot = jnp.where(rows == hit[0:1], one, zero) + jnp.where(rows == hit[1:2], one, zero)
            acc[t * 128 : (t + 1) * 128, :] += jnp.dot(onehot, value, preferred_element_type=F32)

    def source_of(step):
        return (z + nz - offset_of(step, nz)) % nz

    def arrive(step, carry):
        source = source_of(step)
        z_arrival(source).wait_recv()
        forward(source).start()
        before = (z + nz - offset_of((step + nz - 1) % nz, nz)) % nz
        forwarded(before).wait_recv()
        add_rows(before)
        return carry

    lax.fori_loop(0, nz - 1, arrive, 0)
    last = source_of(nz - 2)
    forwarded(last).wait_recv()
    add_rows(last)

    def tile_at(xx, yy):
        return acc[pl.ds(pl.multiple_of((xx * ny + yy) * 128, 128), 128), :]

    def x_copy(j, i):
        return remote(
            xs.at[j, i], xr.at[j, i], xs_sem.at[j, i], xr_sem.at[j, i], x_peer(offset_of(i, nx))
        )

    def send_x(j, carry):
        yy = (y + offset_of(j, ny)) % ny
        for i in range(nx - 1):
            xs[j, i] = tile_at((x + offset_of(i, nx)) % nx, yy).astype(BF16)
            x_copy(j, i).start()
        return carry

    lax.fori_loop(0, ny, send_x, 0)

    def bias_z_wait(step, carry):
        source = source_of(step)
        remote(bias_part.at[0], bias_z.at[source], bzs_sem.at[0], bzr_sem.at[source], sibling).wait_recv()
        return carry

    lax.fori_loop(0, nz - 1, bias_z_wait, 0)
    bias_z[z] = bias_part[z]
    bias_c[core] = jnp.sum(bias_z[...], 0)
    c_copy = remote(bias_c.at[core], bias_c.at[core], bc_sem.at[0], bc_sem.at[1], sibling)
    c_copy.start()

    def y_copy(j):
        return remote(ys.at[j], yr.at[j], ys_sem.at[j], yr_sem.at[j], y_peer(offset_of(j, ny)))

    def sum_x(j):
        yy = (y + offset_of(j, ny)) % ny
        total = tile_at(x, yy)
        for i in range(nx - 1):
            x_copy(j, i).wait_recv()
            total += xr[j, i].astype(F32)
        return total

    def send_y(j, carry):
        ys[j] = sum_x(j).astype(BF16)
        y_copy(j).start()
        return carry

    def bx_copy(i):
        return remote(bias_x.at[x], bias_x.at[x], bxs_sem.at[i], bxr_sem.at[x], x_peer(offset_of(i, nx)))

    def by_copy(j):
        return remote(bias_y.at[y], bias_y.at[y], bys_sem.at[j], byr_sem.at[y], y_peer(offset_of(j, ny)))

    def ba_copy(step):
        return remote(
            bias_all.at[z], bias_all.at[z], bas_sem.at[step], bar_sem.at[z], z_peer(offset_of(step, nz))
        )

    cut = [(ny - 1) * q // 4 for q in range(5)]
    lax.fori_loop(cut[0], cut[1], send_y, 0)

    remote(bias_c.at[core], bias_c.at[1 - core], bc_sem.at[0], bc_sem.at[1], sibling).wait_recv()
    bias_x[x] = bias_c[0] + bias_c[1]
    for i in range(nx - 1):
        bx_copy(i).start()

    lax.fori_loop(cut[1], cut[2], send_y, 0)

    for i in range(nx - 1):
        source = (x + nx - offset_of(i, nx)) % nx
        remote(bias_x.at[x], bias_x.at[source], bxs_sem.at[i], bxr_sem.at[source], sibling).wait_recv()
    bias_y[y] = jnp.sum(bias_x[...], 0)
    lax.fori_loop(0, ny - 1, lambda j, c: (by_copy(j).start(), c)[1], 0)

    lax.fori_loop(cut[2], cut[3], send_y, 0)

    def by_wait(j, carry):
        source = (y + ny - offset_of(j, ny)) % ny
        remote(bias_y.at[y], bias_y.at[source], bys_sem.at[j], byr_sem.at[source], sibling).wait_recv()
        return carry

    lax.fori_loop(0, ny - 1, by_wait, 0)
    bias_all[z] = jnp.sum(bias_y[...], 0)
    lax.fori_loop(0, nz - 1, lambda s, c: (ba_copy(s).start(), c)[1], 0)

    lax.fori_loop(cut[3], cut[4], send_y, 0)

    total = sum_x(ny - 1)
    for j in range(ny - 1):
        y_copy(j).wait_recv()
        total += yr[j].astype(F32)
    row_out[...] = total

    def ba_wait(step, carry):
        source = source_of(step)
        remote(bias_all.at[z], bias_all.at[source], bas_sem.at[0], bar_sem.at[source], sibling).wait_recv()
        return carry

    lax.fori_loop(0, nz - 1, ba_wait, 0)
    for g in range(width // 128):
        bias_out[g : g + 1, :] = bias_all[g // 2, g % 2 : g % 2 + 1, :]

    ids_copy.wait_send()
    c_copy.wait_send()

    def sent_z(step, carry):
        z_copy(step).wait_send()
        bias_z_copy(step).wait_send()
        ba_copy(step).wait_send()
        return carry

    lax.fori_loop(0, nz - 1, sent_z, 0)
    lax.fori_loop(0, nz, lambda s, c: (forward(s).wait_send(), c)[1], 0)

    def sent_y(j, carry):
        y_copy(j).wait_send()
        by_copy(j).wait_send()
        return carry

    lax.fori_loop(0, ny - 1, sent_y, 0)

    def sent_x(j, carry):
        for i in range(nx - 1):
            x_copy(j, i).wait_send()
        return carry

    lax.fori_loop(0, ny, sent_x, 0)
    for i in range(nx - 1):
        bx_copy(i).wait_send()


def body(sizes, features_in, cross_cot, cross_down, cross_up, cross_bias, lookups):
    ny, nx, nz = sizes
    samples, width = features_in.shape[1:]
    rank = cross_down.shape[1]
    tsamp = lookups.shape[2]
    vmem = pl.BlockSpec(memory_space=pltpu.VMEM)
    anywhere = pl.BlockSpec(memory_space=pl.ANY)
    dma = pltpu.SemaphoreType.DMA
    tile = (8, 128)
    bottom, bias, rows = pl.pallas_call(
        functools.partial(kernel, sizes),
        out_shape=(
            jax.ShapeDtypeStruct((samples, EMB), BF16),
            jax.ShapeDtypeStruct((width // 128, 128), F32),
            jax.ShapeDtypeStruct((ROWS_DEV, EMB), F32),
        ),
        in_specs=[anywhere] * 4 + [vmem] * 2,
        out_specs=(vmem, vmem, vmem),
        scratch_shapes=[
            pltpu.VMEM((samples, width), BF16),
            pltpu.VMEM((samples, width), BF16),
            pltpu.VMEM((width, rank), BF16),
            pltpu.VMEM((rank, width), BF16),
            pltpu.VMEM((samples, rank), BF16),
            pltpu.VMEM((samples, rank), BF16),
            pltpu.VMEM((samples, rank), F32),
            pltpu.VMEM((samples, rank), F32),
            pltpu.VMEM((nz - 1, samples, EMB), BF16),
            pltpu.VMEM((nz, 2 * samples, EMB), BF16),
            pltpu.VMEM((CORES, 2, tsamp), jnp.int32),
            pltpu.VMEM((nz, 2, 256), jnp.int32),
            pltpu.VMEM((nz, 2, 256), jnp.int32),
            pltpu.VMEM((nx * ny * ROWS_DEV, EMB), F32),
            pltpu.VMEM((ny, nx - 1, ROWS_DEV, EMB), BF16),
            pltpu.VMEM((ny, nx - 1, ROWS_DEV, EMB), BF16),
            pltpu.VMEM((ny - 1, ROWS_DEV, EMB), BF16),
            pltpu.VMEM((ny - 1, ROWS_DEV, EMB), BF16),
            pltpu.VMEM((nz,) + tile, F32),
            pltpu.VMEM((nz,) + tile, F32),
            pltpu.VMEM((CORES,) + tile, F32),
            pltpu.VMEM((nx,) + tile, F32),
            pltpu.VMEM((ny,) + tile, F32),
            pltpu.VMEM((nz,) + tile, F32),
            dma((4, width // KCHUNK)),
            dma((2,)),
            dma((nz - 1,)),
            dma((nz,)),
            dma((nz,)),
            dma((nz,)),
            dma((ny, nx - 1)),
            dma((ny, nx - 1)),
            dma((ny - 1,)),
            dma((ny - 1,)),
            dma((nz - 1,)),
            dma((nz,)),
            dma((2,)),
            dma((nx - 1,)),
            dma((nx,)),
            dma((ny - 1,)),
            dma((ny,)),
            dma((nz - 1,)),
            dma((nz,)),
        ],
        compiler_params=pltpu.CompilerParams(
            collective_id=0, has_side_effects=True, vmem_limit_bytes=40 << 20
        ),
        name="cross_backward",
    )(
        features_in[0],
        cross_cot[0],
        cross_down,
        cross_up,
        cross_bias.reshape(1, width),
        lookups[0, 0].T,
    )
    return bottom[None], bias.reshape(width), rows[None]


def solution(mesh):
    sizes = (
        mesh.shape["group"] // (XLO * CORES),
        XLO * mesh.shape["batch"],
        mesh.shape["table"],
    )
    placed = (
        P(("group", "batch"), "table", None),
        P(("group", "batch"), "table", None),
        P(),
        P(),
        P(),
        P("table", ("group", "batch"), None, None),
    )
    return jax.shard_map(
        functools.partial(body, sizes),
        mesh=mesh,
        in_specs=placed,
        out_specs=(P(("group", "batch"), "table", None), P(), P("table", ("group", "batch"), None)),
        check_vma=False,
    )
```

time: 380 us -> 95.2 us (0.25)
  waiting for transfers between devices: 161 us -> 0 us
  blocking collectives: 130 us -> 0 us
  Pallas kernels: 0 us -> 84.3 us
  other arithmetic: 28.3 us -> 0 us
  starting transfers between devices: 19.5 us -> 0 us
  between operations: 14.1 us -> 0.65 us
  matrix products: 11.1 us -> 0 us
  local copies, waits for them, and re-layouts: 14.8 us -> 9.63 us
    reduce_scatter x1 -> x0, waiting for transfers between devices: 142 us -> none  [body(): lax.psum_scatter(rows_of(values, own_ids, ROWS_DEV * lax.axis_size(('grou...]
    psum x1 -> x0, blocking collectives: 130 us -> none  [body(): bias_grad = lax.psum(jnp.sum(gate_grad, 0), ('group', 'table', 'batch'))]
    pallas_call x0 -> x1, Pallas kernels: none -> 84.3 us  [body(): pl.pallas_call(functools.partial(kernel, sizes), out_shape=(jax.ShapeDtyp...]
    scatter-add x1 -> x0, other arithmetic: 24.8 us -> none  [rows_of(): return jax.ops.segment_sum(spread, local, num_segments=count + 1)[:count]]
    all_to_all x1 -> x0, starting transfers between devices: 19.5 us -> none  [body(): lax.all_to_all(pooled, 'table', split_axis=1, concat_axis=0, tiled=True)]
    all_to_all x1 -> x0, waiting for transfers between devices: 19 us -> none  [body(): lax.all_to_all(pooled, 'table', split_axis=1, concat_axis=0, tiled=True)]
    dot_general x2 -> x0, matrix products: 11.1 us -> none  [the longest x1 6.13 us: body(): jnp.dot(low_grad, cross_down.T, preferred_element_type=jnp.float32)]
    unnamed x5 -> x13, local copies, waits for them, and re-layouts: 3.37 us -> 8.9 us
  transfers between devices with their start and end apart: 2 -> 0, of which waited for: 2 -> 0; matrix products, arithmetic and copies ran while one was open for 2% -> 0% of each run, Pallas kernels for 0% -> 0%
where the time goes in v1:
time: 95.2 us; the launch traced here: 94.6 us
  Pallas kernels  84.3 us (89%)
  local copies, waits for them, and re-layouts  9.63 us (10%)
    pallas_call x1, Pallas kernels, body(): pl.pallas_call(functools.partial(kernel, sizes), out_shape=(jax.ShapeDtyp...  84.3 us
    unnamed x13, local copies, waits for them, and re-layouts  8.9 us

profile of v1, /device:TPU:1, one launch (start us, length us, event | category | flops | bytes accessed | tf_op | source)
XLA Modules:
  0.0 94.6 jit_solution(12801201372882860735)
XLA Ops:
  0.6 0.7 reshape.12.bias_ref
  1.4 0.0 copy-start
  1.4 2.0 %copy-done = bf16[3456,512]{1,0:T(8,128)(2,1)S(1)} copy-done((bf16[3456,512]{1,0:T(8,128)(2,1)S(1)}, bf16[3456,512]{1,0:T(8,128)(2,1)}, u32[]{:S(2)}) %copy-start) | copy-done | bytes 3538968
  3.4 0.0 copy-start.1
  3.4 2.0 %copy-done.1 = bf16[512,3456]{1,0:T(8,128)(2,1)S(1)} copy-done((bf16[512,3456]{1,0:T(8,128)(2,1)S(1)}, bf16[512,3456]{1,0:T(8,128)(2,1)}, u32[]{:S(2)}) %copy-start.1) | copy-done | bytes 3538968
  5.4 0.0 copy-start.2
  5.4 1.2 %copy-done.2 = bf16[1,128,3456]{2,1,0:T(8,128)(2,1)S(1)} copy-done((bf16[1,128,3456]{2,1,0:T(8,128)(2,1)S(1)}, bf16[1,128,3456]{2,1,0:T(8,128)(2,1)}, u32[]{:S(2)}) %copy-start.2) | copy-done | bytes 884760
  6.5 0.0 copy-start.3
  6.5 1.2 %copy-done.3 = bf16[1,128,3456]{2,1,0:T(8,128)(2,1)S(1)} copy-done((bf16[1,128,3456]{2,1,0:T(8,128)(2,1)S(1)}, bf16[1,128,3456]{2,1,0:T(8,128)(2,1)}, u32[]{:S(2)}) %copy-start.3) | copy-done | bytes 884760
  7.7 0.0 copy-start.4
  7.7 0.7 copy-done.4
  8.4 84.3 %cross_backward.1 = (bf16[128,128]{1,0:T(8,128)(2,1)S(1)}, f32[27,128]{1,0:T(8,128)S(1)}, f32[128,128]{1,0:T(8,128)S(1)}) custom-call(bf16[128,3456]{1,0:T(8,128)(2,1)S(1)} %bitcast.8, bf16[128,3456]{1,0:T(8,128)(2,1)S(1)} %bitcast.9, bf16[3456,512]{1,0:T(8,128)(2,1)S(1)} %copy-done, bf16[512,3456]{1,0:T(8,128)(2,1)S(1)} %copy-done.1, ...), custom_call_target="tpu_custom_call" | custom-call | tf_op jit(solution)/shard_map/cross_backward/pallas_call | solution.py:354
  92.7 0.6 copy.12
  93.4 0.6 copy.13
  94.0 0.6 copy.14
Async XLA Ops:
  1.4 2.0 %copy-start = (bf16[3456,512]{1,0:T(8,128)(2,1)S(1)}, bf16[3456,512]{1,0:T(8,128)(2,1)}, u32[]{:S(2)}) copy-start(bf16[3456,512]{1,0:T(8,128)(2,1)} %down_hbm.1) | copy-start | bytes 10616836
  3.4 2.0 %copy-start.1 = (bf16[512,3456]{1,0:T(8,128)(2,1)S(1)}, bf16[512,3456]{1,0:T(8,128)(2,1)}, u32[]{:S(2)}) copy-start(bf16[512,3456]{1,0:T(8,128)(2,1)} %up_hbm.1) | copy-start | bytes 10616836
  5.4 1.2 %copy-start.2 = (bf16[1,128,3456]{2,1,0:T(8,128)(2,1)S(1)}, bf16[1,128,3456]{2,1,0:T(8,128)(2,1)}, u32[]{:S(2)}) copy-start(bf16[1,128,3456]{2,1,0:T(8,128)(2,1)} %param.6) | copy-start | bytes 2654212
  6.5 1.2 %copy-start.3 = (bf16[1,128,3456]{2,1,0:T(8,128)(2,1)S(1)}, bf16[1,128,3456]{2,1,0:T(8,128)(2,1)}, u32[]{:S(2)}) copy-start(bf16[1,128,3456]{2,1,0:T(8,128)(2,1)} %param.7) | copy-start | bytes 2654212
  7.7 0.7 copy-start.4

commit v2 on v1

v2 whole, which is shorter than its diff:
```python
import functools

import jax
import jax.numpy as jnp
from jax import lax
from jax.experimental import pallas as pl
from jax.experimental.pallas import tpu as pltpu
from jax.sharding import PartitionSpec as P

MESH = pl.DeviceIdType.MESH
F32 = jnp.float32
BF16 = jnp.bfloat16
EMB = 128
ROWS_DEV = 128
XLO = 2
CORES = 2
CUTS = (8, 10, 12, 15)
XLAG = 3
CLAG = 5
KCHUNK = 1152


def offset_of(step, size):
    half = (step + 1) // 2
    odd = step % 2
    return size // 2 + half * (1 - 2 * odd)


def near_of(step, size):
    return offset_of((2 * size - 2 - step) % size, size)


def kernel(
    sizes,
    feat_hbm, cot_hbm, down_hbm, up_hbm, bias_hbm, ids_hbm,
    bottom_ref, bias_out, row_out,
    feat, cot, down, up, bias, low, low_grad, low_acc, grad_acc,
    pooled, vals, ids, tile_of, inner, acc, ys, yr,
    bias_part, bias_z, bias_c, bias_x, bias_y, bias_all,
    load_sem, id_sem, idr_sem, zs_sem, zr_sem, xs_sem, xr_sem, fs_sem, fr_sem, ys_sem, yr_sem,
    bzs_sem, bzr_sem, bc_sem, bxs_sem, bxr_sem, bys_sem, byr_sem, bas_sem, bar_sem,
):
    ny, nx, nz = sizes
    width = feat.shape[1]
    chunks = width // KCHUNK
    group = lax.axis_index("group")
    x_hi = lax.axis_index("batch")
    z = lax.axis_index("table")
    y = group // (XLO * CORES)
    x_lo = (group // CORES) % XLO
    core = group % CORES
    x = x_hi * XLO + x_lo

    def device(xx, yy, zz, cc):
        return {"group": (yy * XLO + xx % XLO) * CORES + cc, "table": zz, "batch": xx // XLO}

    sibling = device(x, y, z, 1 - core)

    def x_peer(offset):
        return device((x + offset) % nx, y, z, core)

    def y_peer(offset):
        return device(x, (y + offset) % ny, z, core)

    def z_peer(offset):
        return device(x, y, (z + offset) % nz, core)

    def remote(src, dst, send, recv, target):
        return pltpu.make_async_remote_copy(
            src_ref=src, dst_ref=dst, send_sem=send, recv_sem=recv, device_id=target, device_id_type=MESH
        )

    def each(count, act):
        lax.fori_loop(0, count, lambda i, c: (act(i), c)[1], 0)

    def loads(k):
        cols = pl.ds(k * KCHUNK, KCHUNK)
        return (
            pltpu.make_async_copy(feat_hbm.at[:, cols], feat.at[:, cols], load_sem.at[0, k]),
            pltpu.make_async_copy(cot_hbm.at[:, cols], cot.at[:, cols], load_sem.at[1, k]),
            pltpu.make_async_copy(down_hbm.at[cols, :], down.at[cols, :], load_sem.at[2, k]),
            pltpu.make_async_copy(up_hbm.at[:, cols], up.at[:, cols], load_sem.at[3, k]),
        )

    for k in range(chunks):
        for copy in loads(k):
            copy.start()
    place = core * nx + x
    load_bias = pltpu.make_async_copy(bias_hbm, bias, load_sem.at[0, chunks])
    load_ids = pltpu.make_async_copy(ids_hbm, ids.at[place], load_sem.at[1, chunks])
    load_bias.start()
    load_ids.start()

    barrier = pltpu.get_barrier_semaphore()

    def greet(target):
        pl.semaphore_signal(barrier, inc=1, device_id=target, device_id_type=MESH)

    each(nz - 1, lambda i: greet(z_peer(offset_of(i, nz))))
    each(ny - 1, lambda i: greet(y_peer(offset_of(i, ny))))
    for offset in range(1, nx):
        greet(x_peer(offset))
        greet(device((x + offset) % nx, y, z, 1 - core))
    greet(sibling)

    acc[...] = jnp.zeros_like(acc)
    bias_part[...] = jnp.zeros_like(bias_part)

    for k in range(chunks):
        for copy in loads(k):
            copy.wait()
        cols = slice(k * KCHUNK, (k + 1) * KCHUNK)
        part_in = feat[:, cols]
        gate_grad = cot[:, cols].astype(F32) * part_in.astype(F32)
        sums = jnp.sum(gate_grad, 0, keepdims=True)
        for j in range(KCHUNK // 128):
            g = k * (KCHUNK // 128) + j
            bias_part[g // 2, g % 2 : g % 2 + 1, :] = sums[:, j * 128 : (j + 1) * 128]
        first = jnp.dot(part_in, down[cols, :], preferred_element_type=F32)
        second = lax.dot_general(
            gate_grad.astype(BF16), up[:, cols], (((1,), (1,)), ((), ())), preferred_element_type=F32
        )
        if k == 0:
            low_acc[...] = first
            grad_acc[...] = second
        else:
            low_acc[...] += first
            grad_acc[...] += second
    low[...] = low_acc[...].astype(BF16)
    low_grad[...] = grad_acc[...].astype(BF16)
    load_bias.wait()
    load_ids.wait()

    def columns(start, count):
        cols = slice(start, start + count)
        gate = jnp.dot(low[...], up[:, cols], preferred_element_type=F32) + bias[cols].reshape(1, count)
        back = lax.dot_general(
            low_grad[...], down[cols, :], (((1,), (1,)), ((), ())), preferred_element_type=F32
        )
        return (cot[:, cols].astype(F32) * (gate + 1.0) + back).astype(BF16)

    for f in range(0, nz, 2):
        pair = columns(128 + f * 128, 256)
        pooled[f] = pair[:, :128]
        pooled[f + 1] = pair[:, 128:]

    pl.semaphore_wait(barrier, (nz - 1) + (ny - 1) + 2 * (nx - 1) + 1)

    def bias_z_copy(step):
        offset = near_of(step, nz)
        return remote(
            bias_part.at[(z + offset) % nz], bias_z.at[z], bzs_sem.at[step], bzr_sem.at[z], z_peer(offset)
        )

    each(nz - 1, lambda s: bias_z_copy(s).start())

    mine = pl.ds(pl.multiple_of(x * 128, 128), 128)

    def z_copy(step):
        offset = near_of(step, nz)
        return remote(
            pooled.at[(z + offset) % nz], vals.at[z, core, mine], zs_sem.at[step], zr_sem.at[z], z_peer(offset)
        )

    each(nz - 1, lambda s: z_copy(s).start())

    def id_copy(i):
        if i == nx - 1:
            target = sibling
        elif i < nx - 1:
            target = x_peer(i + 1)
        else:
            target = device((x + i - nx + 1) % nx, y, z, 1 - core)
        return remote(ids.at[place], ids.at[place], id_sem.at[i], idr_sem.at[place], target)

    for i in range(2 * nx - 1):
        id_copy(i).start()

    vals[z, core, mine] = pooled[z]

    def source_of(step):
        return (z + nz - near_of(step, nz)) % nz

    def z_wait(source):
        remote(pooled.at[0], vals.at[source, core, mine], zs_sem.at[0], zr_sem.at[source], sibling).wait_recv()

    def x_copy(source, i):
        spot = vals.at[source, core, mine]
        return remote(spot, spot, xs_sem.at[source, i], xr_sem.at[source, x], x_peer(offset_of(i, nx)))

    def x_send(source):
        for i in range(nx - 1):
            x_copy(source, i).start()

    def x_wait(source):
        for i in range(nx - 1):
            there = (x + nx - offset_of(i, nx)) % nx
            spot = vals.at[source, core, pl.ds(pl.multiple_of(there * 128, 128), 128)]
            remote(spot, spot, xs_sem.at[source, i], xr_sem.at[source, there], sibling).wait_recv()

    def core_copy(source):
        spot = vals.at[source, core]
        return remote(spot, spot, fs_sem.at[source], fr_sem.at[source], sibling)

    def core_wait(source):
        spot = vals.at[source, 1 - core]
        remote(spot, spot, fs_sem.at[source], fr_sem.at[source], sibling).wait_recv()

    x_send(z)

    bottom_ref[...] = columns(0, 128)

    for c in range(CORES):
        for xx in range(nx):
            k = c * nx + xx

            @pl.when(k != place)
            def _():
                remote(ids.at[k], ids.at[k], id_sem.at[0], idr_sem.at[k], sibling).wait_recv()

            row = ids[k]
            block = row >> 7
            here = (((block >> 1) & 1) == core) & ((block & 1) == x_hi) & (((block >> 2) & 1) == x_lo)
            tile_of[2 * k : 2 * k + 2, :] = jnp.where(here, block >> 3, -1)
            inner[2 * k : 2 * k + 2, :] = row & 127

    def products(source, tiles):
        part = pl.ds(pl.multiple_of(source * 128, 128), 128)
        tile_here, inner_here = tile_of[:, part], inner[:, part]
        value = vals[source].reshape(CORES * nx * 128, EMB)
        rows = lax.broadcasted_iota(jnp.int32, (ROWS_DEV, 128), 0).astype(F32).astype(BF16)
        one, zero = jnp.ones((), BF16), jnp.zeros((), BF16)
        for t in tiles:
            hit = jnp.where(tile_here == t, inner_here, -1).astype(F32).astype(BF16)
            onehot = jnp.concatenate(
                [
                    jnp.where(rows == hit[2 * k : 2 * k + 1], one, zero)
                    + jnp.where(rows == hit[2 * k + 1 : 2 * k + 2], one, zero)
                    for k in range(CORES * nx)
                ],
                1,
            )
            yield t, jnp.dot(onehot, value, preferred_element_type=F32)

    def add_rows(source):
        for t, product in products(source, range(ny)):
            acc[t * 128 : (t + 1) * 128, :] += product

    def nth(k):
        return source_of((k + nz - 1) % nz)

    def arrive(k):
        z_wait(nth(k))
        x_send(nth(k))

    def gather(k):
        x_wait(nth(k))
        core_copy(nth(k)).start()

    def add(k):
        core_wait(nth(k))
        add_rows(nth(k))

    def all_three(k, carry):
        arrive(k)
        gather(k - XLAG)
        add(k - CLAG)
        return carry

    for k in range(1, CLAG):
        arrive(k)
        if k >= XLAG:
            gather(k - XLAG)

    lax.fori_loop(CLAG, CUTS[0], all_three, 0)

    def bias_z_wait(step):
        source = source_of(step)
        remote(bias_part.at[0], bias_z.at[source], bzs_sem.at[0], bzr_sem.at[source], sibling).wait_recv()

    each(nz - 1, bias_z_wait)
    bias_z[z] = bias_part[z]
    bias_c[core] = jnp.sum(bias_z[...], 0)
    c_copy = remote(bias_c.at[core], bias_c.at[core], bc_sem.at[0], bc_sem.at[1], sibling)
    c_copy.start()

    lax.fori_loop(CUTS[0], CUTS[1], all_three, 0)

    def bx_copy(i):
        return remote(bias_x.at[x], bias_x.at[x], bxs_sem.at[i], bxr_sem.at[x], x_peer(offset_of(i, nx)))

    def by_copy(j):
        return remote(bias_y.at[y], bias_y.at[y], bys_sem.at[j], byr_sem.at[y], y_peer(offset_of(j, ny)))

    def ba_copy(step):
        return remote(
            bias_all.at[z], bias_all.at[z], bas_sem.at[step], bar_sem.at[z], z_peer(near_of(step, nz))
        )

    remote(bias_c.at[core], bias_c.at[1 - core], bc_sem.at[0], bc_sem.at[1], sibling).wait_recv()
    bias_x[x] = bias_c[0] + bias_c[1]
    for i in range(nx - 1):
        bx_copy(i).start()

    lax.fori_loop(CUTS[1], CUTS[2], all_three, 0)

    for i in range(nx - 1):
        source = (x + nx - offset_of(i, nx)) % nx
        remote(bias_x.at[x], bias_x.at[source], bxs_sem.at[i], bxr_sem.at[source], sibling).wait_recv()
    bias_y[y] = jnp.sum(bias_x[...], 0)
    each(ny - 1, lambda j: by_copy(j).start())

    lax.fori_loop(CUTS[2], CUTS[3], all_three, 0)

    def by_wait(j):
        source = (y + ny - offset_of(j, ny)) % ny
        remote(bias_y.at[y], bias_y.at[source], bys_sem.at[j], byr_sem.at[source], sibling).wait_recv()

    each(ny - 1, by_wait)
    bias_all[z] = jnp.sum(bias_y[...], 0)
    each(nz - 1, lambda s: ba_copy(s).start())

    lax.fori_loop(CUTS[3], nz, all_three, 0)

    for k in range(nz, nz + CLAG - 1):
        if k - XLAG < nz:
            gather(k - XLAG)
        add(k - CLAG)
    last = nth(nz - 1)
    core_wait(last)

    def y_copy(j):
        return remote(ys.at[j], yr.at[j], ys_sem.at[j], yr_sem.at[j], y_peer(offset_of(j, ny)))

    order = [(y + offset_of(j, ny)) % ny for j in range(ny)]
    total = None
    for j, (t, product) in enumerate(products(last, order)):
        whole = acc[pl.ds(pl.multiple_of(t * 128, 128), 128), :] + product
        if j < ny - 1:
            ys[j] = whole.astype(BF16)
            y_copy(j).start()
        else:
            total = whole

    for i in range(2 * nx - 1):
        id_copy(i).wait_send()
    c_copy.wait_send()
    for i in range(nx - 1):
        bx_copy(i).wait_send()
    each(ny - 1, lambda j: by_copy(j).wait_send())

    def sent_z(step):
        z_copy(step).wait_send()
        bias_z_copy(step).wait_send()

    def sent_block(source):
        for i in range(nx - 1):
            x_copy(source, i).wait_send()
        core_copy(source).wait_send()

    each(nz - 1, sent_z)
    each(nz, sent_block)

    def ba_wait(step):
        source = source_of(step)
        remote(bias_all.at[z], bias_all.at[source], bas_sem.at[0], bar_sem.at[source], sibling).wait_recv()
        ba_copy(step).wait_send()

    each(nz - 1, ba_wait)
    for g in range(width // 128):
        bias_out[g : g + 1, :] = bias_all[g // 2, g % 2 : g % 2 + 1, :]

    for j in range(ny - 1):
        y_copy(j).wait_recv()
        total += yr[j].astype(F32)
    row_out[...] = total
    each(ny - 1, lambda j: y_copy(j).wait_send())


def body(sizes, features_in, cross_cot, cross_down, cross_up, cross_bias, lookups):
    ny, nx, nz = sizes
    samples, width = features_in.shape[1:]
    rank = cross_down.shape[1]
    tsamp = lookups.shape[2]
    group = CORES * nx
    vmem = pl.BlockSpec(memory_space=pltpu.VMEM)
    anywhere = pl.BlockSpec(memory_space=pl.ANY)
    dma = pltpu.SemaphoreType.DMA
    bottom, bias, rows = pl.pallas_call(
        functools.partial(kernel, sizes),
        out_shape=(
            jax.ShapeDtypeStruct((samples, EMB), BF16),
            jax.ShapeDtypeStruct((width // 128, 128), F32),
            jax.ShapeDtypeStruct((ROWS_DEV, EMB), F32),
        ),
        in_specs=[anywhere] * 6,
        out_specs=(vmem, vmem, vmem),
        scratch_shapes=[
            pltpu.VMEM((samples, width), BF16),
            pltpu.VMEM((samples, width), BF16),
            pltpu.VMEM((width, rank), BF16),
            pltpu.VMEM((rank, width), BF16),
            pltpu.VMEM((width,), F32),
            pltpu.VMEM((samples, rank), BF16),
            pltpu.VMEM((samples, rank), BF16),
            pltpu.VMEM((samples, rank), F32),
            pltpu.VMEM((samples, rank), F32),
            pltpu.VMEM((nz, samples, EMB), BF16),
            pltpu.VMEM((nz, CORES, nx * samples, EMB), BF16),
            pltpu.VMEM((group, 2, tsamp), jnp.int32),
            pltpu.VMEM((2 * group, tsamp), jnp.int32),
            pltpu.VMEM((2 * group, tsamp), jnp.int32),
            pltpu.VMEM((ny * ROWS_DEV, EMB), F32),
            pltpu.VMEM((ny - 1, ROWS_DEV, EMB), BF16),
            pltpu.VMEM((ny - 1, ROWS_DEV, EMB), BF16),
            pltpu.VMEM((nz, 2, 128), F32),
            pltpu.VMEM((nz, 2, 128), F32),
            pltpu.VMEM((CORES, 2, 128), F32),
            pltpu.VMEM((nx, 2, 128), F32),
            pltpu.VMEM((ny, 2, 128), F32),
            pltpu.VMEM((nz, 2, 128), F32),
            dma((4, width // KCHUNK + 1)),
            dma((2 * nx - 1,)),
            dma((2 * nx,)),
            dma((nz - 1,)),
            dma((nz,)),
            dma((nz, nx - 1)),
            dma((nz, nx)),
            dma((nz,)),
            dma((nz,)),
            dma((ny - 1,)),
            dma((ny - 1,)),
            dma((nz - 1,)),
            dma((nz,)),
            dma((2,)),
            dma((nx - 1,)),
            dma((nx,)),
            dma((ny - 1,)),
            dma((ny,)),
            dma((nz - 1,)),
            dma((nz,)),
        ],
        compiler_params=pltpu.CompilerParams(
            collective_id=0, has_side_effects=True, vmem_limit_bytes=62 << 20
        ),
        name="cross_backward",
    )(
        features_in[0],
        cross_cot[0],
        cross_down,
        cross_up,
        cross_bias,
        lookups[0, 0].T,
    )
    return bottom[None], bias.reshape(width), rows[None]


def solution(mesh):
    sizes = (
        mesh.shape["group"] // (XLO * CORES),
        XLO * mesh.shape["batch"],
        mesh.shape["table"],
    )
    placed = (
        P(("group", "batch"), "table", None),
        P(("group", "batch"), "table", None),
        P(),
        P(),
        P(),
        P("table", ("group", "batch"), None, None),
    )
    return jax.shard_map(
        functools.partial(body, sizes),
        mesh=mesh,
        in_specs=placed,
        out_specs=(P(("group", "batch"), "table", None), P(), P("table", ("group", "batch"), None)),
        check_vma=False,
    )
```

time: 95.2 us -> 77.4 us (0.81)
  Pallas kernels: 84.3 us -> 72.2 us
  local copies, waits for them, and re-layouts: 9.63 us -> 4.17 us
    pallas_call x1, Pallas kernels: 84.3 us -> 72.2 us  [body(): pl.pallas_call(functools.partial(kernel, sizes), out_shape=(jax.ShapeDtyp...]
    unnamed x13 -> x3, local copies, waits for them, and re-layouts: 8.9 us -> 4.17 us
where the time goes in v2:
time: 77.4 us; the launch traced here: 77.1 us
  Pallas kernels  72.2 us (93%)
  local copies, waits for them, and re-layouts  4.17 us (5%)
    pallas_call x1, Pallas kernels, body(): pl.pallas_call(functools.partial(kernel, sizes), out_shape=(jax.ShapeDtyp...  72.2 us
    unnamed x3, local copies, waits for them, and re-layouts  4.17 us

profile of v2, /device:TPU:1, one launch (start us, length us, event | category | flops | bytes accessed | tf_op | source)
XLA Modules:
  0.0 77.1 jit_solution(8304914793450154668)
XLA Ops:
  0.6 72.2 %cross_backward.1 = (bf16[128,128]{1,0:T(8,128)(2,1)}, f32[27,128]{1,0:T(8,128)}, f32[128,128]{1,0:T(8,128)}) custom-call(bf16[128,3456]{1,0:T(8,128)(2,1)} %bitcast.8, bf16[128,3456]{1,0:T(8,128)(2,1)} %bitcast.9, bf16[3456,512]{1,0:T(8,128)(2,1)} %down_hbm.1, bf16[512,3456]{1,0:T(8,128)(2,1)} %up_hbm.1, f32[3456]{0:T(1024)} %bias_hbm.1, s32[2,2048]{1,0:T(2,128)} %bitcast.12), custom_call_target="tpu_custom_call" | custom-call | tf_op jit(solution)/shard_map/cross_backward/pallas_call | solution.py:389
  72.9 1.4 %copy.12 = bf16[1,128,128]{2,1,0:T(8,128)(2,1)} copy(bf16[1,128,128]{2,1,0:T(8,128)(2,1)} %bitcast.11) | data formatting | bytes 65536
  74.3 1.3 %copy.13 = f32[3456]{0:T(1024)} copy(f32[3456]{0:T(1024)} %bitcast.13) | data formatting | bytes 27648
  75.6 1.5 %copy.14 = f32[1,128,128]{2,1,0:T(8,128)} copy(f32[1,128,128]{2,1,0:T(8,128)} %bitcast.10) | data formatting | bytes 131072

commit v3 on v2

--- a/solution.py
+++ b/solution.py
@@ -14,7 +14,7 @@
 ROWS_DEV = 128
 XLO = 2
 CORES = 2
-CUTS = (8, 10, 12, 15)
+CUTS = (5, 6, 7, 9)
 XLAG = 3
 CLAG = 5
 KCHUNK = 1152
@@ -441,7 +441,7 @@
             dma((nz,)),
         ],
         compiler_params=pltpu.CompilerParams(
-            collective_id=0, has_side_effects=True, vmem_limit_bytes=62 << 20
+            collective_id=0, has_side_effects=True, vmem_limit_bytes=53 << 20
         ),
         name="cross_backward",
     )(

time: 77.4 us -> 74.4 us (0.961); the launches traced: 77.1 us -> 73.1 us
  Pallas kernels: 72.2 us -> 69.1 us
  local copies, waits for them, and re-layouts: 4.17 us -> 3.28 us
    pallas_call x1, Pallas kernels: 72.2 us -> 69.1 us  [body(): pl.pallas_call(functools.partial(kernel, sizes), out_shape=(jax.ShapeDtyp...]
    unnamed x3 -> x7, local copies, waits for them, and re-layouts: 4.17 us -> 3.28 us
where the time goes in v3:
time: 74.4 us; the launch traced here: 73.1 us
  Pallas kernels  69.1 us (93%)
  local copies, waits for them, and re-layouts  3.28 us (4%)
    pallas_call x1, Pallas kernels, body(): pl.pallas_call(functools.partial(kernel, sizes), out_shape=(jax.ShapeDtyp...  69.1 us
    unnamed x7, local copies, waits for them, and re-layouts  3.28 us

profile of v3, /device:TPU:1, one launch (start us, length us, event | category | flops | bytes accessed | tf_op | source)
XLA Modules:
  0.0 73.1 jit_solution(6657291518315956244)
XLA Ops:
  0.6 0.0 copy-start
  0.6 0.7 copy-done
  1.4 0.0 copy-start.1
  1.4 0.7 copy-done.1
  2.1 69.1 %cross_backward.1 = (bf16[128,128]{1,0:T(8,128)(2,1)S(1)}, f32[27,128]{1,0:T(8,128)S(1)}, f32[128,128]{1,0:T(8,128)S(1)}) custom-call(bf16[128,3456]{1,0:T(8,128)(2,1)} %bitcast.12, bf16[128,3456]{1,0:T(8,128)(2,1)} %bitcast.13, bf16[3456,512]{1,0:T(8,128)(2,1)} %down_hbm.1, bf16[512,3456]{1,0:T(8,128)(2,1)} %up_hbm.1, f32[3456]{0:T(1024)S(1)} %copy-done, ...), custom_call_target="tpu_custom_call" | custom-call | tf_op jit(solution)/shard_map/cross_backward/pallas_call | solution.py:389
  71.2 0.6 copy.12
  71.8 0.6 copy.13
  72.4 0.6 copy.14
Async XLA Ops:
  0.6 0.7 copy-start
  1.4 0.7 copy-start.1
